TPU v7x, 256 devices: a whole 4x4x8 slice. The times are simulated.
256 devices in a mesh: ctx: 64 (over x, y_lo, z), tp: 4 (over y_hi, core).
Axes of the slice: x: 4, y: 4 (y_hi: 2, y_lo: 2; y = y_hi * 2 + y_lo), z: 8, core: 2. Of those that a mesh axis runs over, the one named last changes fastest.
Arguments:
- queries: bfloat16 [12288, 4096], P('ctx', 'tp'), may hold values from -40 to 40
- prompt_window_keys: bfloat16 [12288, 512], P('ctx', 'tp'), may hold values from -10 to 10
- prompt_window_values: bfloat16 [12288, 512], P('ctx', 'tp'), may hold values from -6 to 6
- stored_keys: bfloat16 [4096, 512], P('ctx', 'tp'), may hold values from -4 to 4
- stored_values: bfloat16 [4096, 512], P('ctx', 'tp'), may hold values from -6 to 6
- block_order: int32 [128], replicated, may hold values from 0 to 127, as said below
- window_offset: int32 [1], replicated, may hold values from 1024 to 4096
- out_weight: bfloat16 [4096, 4096], P('tp'), may hold values from -0.25 to 0.25
Outputs:
- projected: bfloat16 [12288, 4096], P(('ctx', 'tp'))
Inputs may be any that keep to these rules, and one draw needn't show every extreme that they name: `block_order`: block slots 2d and 2d + 1 (the rows of index d of ctx) hold two window blocks whose numbers add up to 127; every block appears once.
All inputs are finite; a program needn't handle non-finite values.
Results may differ from a plain program's by a relative error of at most 0.015.
Values may be sent and summed in bfloat16 or wider, within the bound.
No kernel may reach another device: no remote copies, remote signals or barrier semaphores. Data moves between devices by JAX's collectives and lax.ppermute only.
A program may use at most 64 MiB of HBM per device.

v0:
```python
import jax
import jax.numpy as jnp
from jax import lax
from jax.sharding import PartitionSpec as P

QUERY_HEADS = 32
KEY_VALUE_HEADS = 4
HEAD_SIZE = 128


masked_score = -1e30
tile_rows = 512


def block_positions(block_order, block_index, within_block, block_rows):
    block_ids = jnp.arange(block_order.shape[0], dtype=jnp.int32)
    picked = jnp.sum(
        jnp.where(block_index[:, None] == block_ids[None, :], block_order[None, :], 0), axis=1
    )
    return picked * block_rows + within_block


def visibility(query_pos, inside, window_pos, cache_pos, offset):
    return jnp.where(
        inside[None, :], window_pos[None, :] <= query_pos[:, None], (cache_pos < offset)[None, :]
    )


def attend(current, query_tile, key_tile, value_tile, visible, score_scale):
    run_max, run_sum, run_acc = current
    local_heads = query_tile.shape[0]
    key_heads = key_tile.reshape(key_tile.shape[0], local_heads, -1)
    value_heads = value_tile.reshape(value_tile.shape[0], local_heads, -1)
    scores = (
        jnp.einsum("grd,ngd->grn", query_tile, key_heads, preferred_element_type=jnp.float32)
        * score_scale
    )
    scores = jnp.where(visible[None], scores, masked_score)
    new_max = jnp.maximum(run_max, jnp.max(scores, axis=-1))
    factor = jnp.exp(run_max - new_max)
    weights = jnp.where(visible[None], jnp.exp(scores - new_max[..., None]), 0.0)
    new_sum = run_sum * factor + jnp.sum(weights, axis=-1)
    mixed = jnp.einsum(
        "grn,ngd->grd",
        weights.astype(jnp.bfloat16),
        value_heads,
        preferred_element_type=jnp.float32,
    )
    new_acc = run_acc * factor[..., None] + mixed
    return (new_max, new_sum, new_acc)


def on_device(
    queries,
    prompt_window_keys,
    prompt_window_values,
    stored_keys,
    stored_values,
    block_order,
    window_offset,
    out_weight,
):
    token_count = queries.shape[0]
    block_rows = token_count // 2
    cache_slots = stored_keys.shape[0]
    local_heads = prompt_window_keys.shape[1] // HEAD_SIZE
    group_split = QUERY_HEADS // KEY_VALUE_HEADS
    score_scale = HEAD_SIZE ** (-0.5)
    offset = window_offset[0]
    device = lax.axis_index("ctx")
    my_blocks = lax.dynamic_slice_in_dim(block_order, device * 2, 2)
    grouped = queries.reshape(2, block_rows, local_heads, group_split, HEAD_SIZE).transpose(
        0, 2, 1, 3, 4
    )
    grouped = grouped.reshape(2, local_heads, block_rows * group_split, HEAD_SIZE)
    row_ids = jnp.arange(block_rows * group_split, dtype=jnp.int32) // group_split
    query_pos = (my_blocks[0] * block_rows + row_ids, my_blocks[1] * block_rows + row_ids)
    query_count = block_rows * group_split
    start_one = (
        jnp.full((local_heads, query_count), masked_score, jnp.float32),
        jnp.zeros((local_heads, query_count), jnp.float32),
        jnp.zeros((local_heads, query_count, HEAD_SIZE), jnp.float32),
    )
    start_states = (start_one, start_one)

    def positions(first_row, row_count, shard_rows):
        global_row = first_row + jnp.arange(row_count, dtype=jnp.int32)
        owner_index = global_row // shard_rows
        local_row = global_row % shard_rows
        inside = local_row < token_count
        cache_pos = owner_index * cache_slots + local_row - token_count
        block_index = owner_index * 2 + jnp.minimum(local_row // block_rows, 1)
        window_pos = block_positions(block_order, block_index, local_row % block_rows, block_rows)
        return (inside, window_pos, cache_pos)

    def absorb(states, key_tile, value_tile, inside, window_pos, cache_pos):
        updated = []
        for qblock in range(2):
            visible = visibility(query_pos[qblock], inside, window_pos, cache_pos, offset)

            def compute(current, qblock=qblock, visible=visible):
                return attend(current, grouped[qblock], key_tile, value_tile, visible, score_scale)

            updated.append(compute(states[qblock]))
        return tuple(updated)

    stacked_keys = jnp.concatenate([prompt_window_keys, stored_keys], 0)
    stacked_values = jnp.concatenate([prompt_window_values, stored_values], 0)
    states = start_states
    key_rows = lax.all_gather(stacked_keys, "ctx", axis=0, tiled=True)
    value_rows = lax.all_gather(stacked_values, "ctx", axis=0, tiled=True)
    shard_rows = token_count + cache_slots
    row_count = key_rows.shape[0]
    full_tiles = row_count // tile_rows
    shaped_keys = key_rows.reshape(full_tiles, tile_rows, key_rows.shape[1])
    shaped_values = value_rows.reshape(full_tiles, tile_rows, value_rows.shape[1])
    starts = jnp.arange(full_tiles, dtype=jnp.int32) * tile_rows

    def tile_step(current, pieces):
        tile_keys, tile_values, tile_start = pieces
        inside, window_pos, cache_pos = positions(tile_start, tile_rows, shard_rows)
        return (absorb(current, tile_keys, tile_values, inside, window_pos, cache_pos), None)

    states, ignored = lax.scan(tile_step, states, (shaped_keys, shaped_values, starts))
    blocks_out = []
    for qblock in range(2):
        run_max, run_sum, run_acc = states[qblock]
        blocks_out.append(run_acc / run_sum[..., None])
    attended = jnp.stack(blocks_out).astype(jnp.bfloat16)
    attended = attended.reshape(2, local_heads, block_rows, group_split, HEAD_SIZE).transpose(
        0, 2, 1, 3, 4
    )
    attended = attended.reshape(token_count, local_heads * group_split * HEAD_SIZE)
    tp_count = lax.axis_size("tp")
    share_rows = token_count // tp_count
    summed = lax.psum(
        jnp.dot(attended, out_weight, preferred_element_type=jnp.float32).astype(jnp.bfloat16), "tp"
    ).astype(jnp.float32)
    picked = lax.dynamic_slice_in_dim(summed, lax.axis_index("tp") * share_rows, share_rows, 0)
    return picked.astype(jnp.bfloat16)


def solution(mesh):
    return jax.shard_map(
        on_device,
        mesh=mesh,
        in_specs=(
            P("ctx", "tp"),
            P("ctx", "tp"),
            P("ctx", "tp"),
            P("ctx", "tp"),
            P("ctx", "tp"),
            P(),
            P(),
            P("tp", None),
        ),
        out_specs=P(("ctx", "tp"), None),
        check_vma=False,
    )
```

profile of v0, /device:TPU:1, one launch (start us, length us, event | category | flops | bytes accessed | tf_op | source)
XLA Modules:
  0.0 1074.3 jit_solution(9587900062713825992)
XLA Ops:
  13.5 260.5 %all-gather.3.cloned.1.call-done = bf16[16384,128]{1,0:T(8,128)(2,1)} async-done(((bf16[256,128]{1,0:T(8,128)(2,1)}), bf16[16384,128]{1,0:T(8,128)(2,1)}) %all-gather.3.cloned.1.call-update) | async-done | bytes 4194320 | tf_op jit(solution)/shard_map/all_gather | solution.py:110
  274.0 302.9 %all-gather.5.cloned.1.call-done = bf16[16384,128]{1,0:T(8,128)(2,1)} async-done(((bf16[256,128]{1,0:T(8,128)(2,1)}), bf16[16384,128]{1,0:T(8,128)(2,1)}) %all-gather.5.cloned.1.call-update) | async-done | bytes 4194320 | tf_op jit(solution)/shard_map/all_gather | solution.py:111
  576.9 385.3 %while.24 = (s32[]{:T(128)}, f32[1,768]{1,0:T(1,128)S(1)}, f32[1,768]{1,0:T(1,128)S(1)}, f32[1,768,128]{2,1,0:T(8,128)S(1)}, f32[1,768]{1,0:T(1,128)S(1)}, /*ind...) while((s32[]{:T(128)}, f32[1,768]{1,0:T(1,128)S(1)}, ...), condition=%wide.region_6.7_spmd.clone, body=%wide.region_0.6_spmd.clone.sunk | while | flops 415291392 | bytes 12088016 | solution.py:124
  582.5 1.8 fusion.94
  587.1 1.8 fusion.92
  594.6 1.8 fusion.94
  599.1 1.8 fusion.92
  606.6 1.8 fusion.94
  611.2 1.8 fusion.92
  618.7 1.8 fusion.94
  623.2 1.8 fusion.92
  630.7 1.8 fusion.94
  635.3 1.8 fusion.92
  642.8 1.8 fusion.94
  647.3 1.8 fusion.92
  654.8 1.8 fusion.94
  659.4 1.8 fusion.92
  666.8 1.8 fusion.94
  671.4 1.8 fusion.92
  678.9 1.8 fusion.94
  683.4 1.8 fusion.92
  690.9 1.8 fusion.94
  695.5 1.8 fusion.92
  703.0 1.8 fusion.94
  707.5 1.8 fusion.92
  715.0 1.8 fusion.94
  719.6 1.8 fusion.92
  727.1 1.8 fusion.94
  731.6 1.8 fusion.92
  739.1 1.8 fusion.94
  743.7 1.8 fusion.92
  751.1 1.8 fusion.94
  755.7 1.8 fusion.92
  763.2 1.8 fusion.94
  767.7 1.8 fusion.92
  775.2 1.8 fusion.94
  779.8 1.8 fusion.92
  787.3 1.8 fusion.94
  791.8 1.8 fusion.92
  799.3 1.8 fusion.94
  803.9 1.8 fusion.92
  811.4 1.8 fusion.94
  815.9 1.8 fusion.92
  823.4 1.8 fusion.94
  827.9 1.8 fusion.92
  835.4 1.8 fusion.94
  840.0 1.8 fusion.92
  847.5 1.8 fusion.94
  852.0 1.8 fusion.92
  859.5 1.8 fusion.94
  864.1 1.8 fusion.92
  871.6 1.8 fusion.94
  876.1 1.8 fusion.92
  888.2 1.8 fusion.92
  900.2 1.8 fusion.92
  912.2 1.8 fusion.92
  919.7 1.8 fusion.94
  924.3 1.8 fusion.92
  936.3 1.8 fusion.92
  948.4 1.8 fusion.92
  955.9 1.8 fusion.94
  960.4 1.8 fusion.92
  962.8 6.3 convolution_convert_fusion
  969.2 96.8 %all-reduce.2.cloned.1.call-done = bf16[192,4096]{1,0:T(8,128)(2,1)} async-done(((bf16[192,4096]{1,0:T(8,128)(2,1)}), bf16[192,4096]{1,0:T(8,128)(2,1)}) %all-reduce.2.cloned.1.call-update) | async-done | bytes 1572880 | tf_op jit(solution)/shard_map/psum | solution.py:136
  (509 shorter events, 285.3 us)
Async XLA Ops:
  6.5 267.4 %all-gather.3.cloned.1.call-start = ((), (), s32[]{:S(2)}) async-start(), calls=%async_computation | async-start | bytes 4259840 | tf_op jit(solution)/shard_map/all_gather | solution.py:110
  8.0 568.9 %all-gather.5.cloned.1.call-start = ((), (), s32[]{:S(2)}) async-start(), calls=%async_computation.1 | async-start | bytes 4259840 | tf_op jit(solution)/shard_map/all_gather | solution.py:111
  9.5 1056.4 %all-reduce.2.cloned.1.call-start = ((), (), s32[]{:S(2)}) async-start(), calls=%async_computation.2 | async-start | bytes 3145728 | tf_op jit(solution)/shard_map/psum | solution.py:136
Sparse Core Ops, SparseCore 0:
  9.1 264.7 all-gather.2
  275.8 301.0 all-gather.4
  969.3 96.6 all-reduce.1
where the time goes:
time: 1080 us; the launch traced here: 1070 us
  waiting for transfers between devices  660 us (61%)
  matrix products  213 us (20%)
  other arithmetic  161 us (15%)
  local copies, waits for them, and re-layouts  21.6 us (2%)
  between operations  14.5 us (1%)
    all_gather x1, waiting for transfers between devices, on_device(): value_rows = lax.all_gather(stacked_values, 'ctx', axis=0, tiled=True)  303 us
    all_gather x1, waiting for transfers between devices, on_device(): key_rows = lax.all_gather(stacked_keys, 'ctx', axis=0, tiled=True)  260 us
    dot_general x64, matrix products, attend(): jnp.einsum('grn,ngd->grd', weights.astype(jnp.bfloat16), value_heads, pre...  113 us
    psum x1, waiting for transfers between devices, on_device(): lax.psum(jnp.dot(attended, out_weight, preferred_element_type=jnp.float32...  96.8 us
    dot_general x64, matrix products, attend(): jnp.einsum('grd,ngd->grn', query_tile, key_heads, preferred_element_type=...  93.4 us
    lt x32, other arithmetic, visibility(): cache_pos < offset  41.9 us
    reduce_sum x32, other arithmetic, attend(): new_sum = run_sum * factor + jnp.sum(weights, axis=-1)  39.8 us
    reduce_sum x32, other arithmetic, block_positions(): jnp.sum(jnp.where(block_index[:, None] == block_ids[None, :], block_order...  28.4 us
  transfers between devices with their start and end apart: 3, of which 3 were waited for; matrix products, arithmetic and copies ran while one was open for 0% of the time, Pallas kernels for 0%

commit v1 on v0

v1 whole, which is shorter than its diff:
```python
import functools

import jax
import jax.numpy as jnp
from jax import lax
from jax.experimental import pallas as pl
from jax.experimental.pallas import tpu as pltpu
from jax.sharding import Mesh, PartitionSpec as P

HEADS = 8
D = 128
BLK = 96
TOK = 2 * BLK
CACHE = 64
SHARD = 2 * (TOK + CACHE)
ROWS = HEADS * BLK
TILE = 512
NEG = -1e30
SCALE = D**-0.5 * 1.4426950408889634
OUT_ROWS = D + 16
NT = (((1,), (1,)), ((), ()))
TN = (((0,), (0,)), ((), ()))
VMEM = pltpu.VMEM


def attend_chunk(steps, first, last, *refs):
    refs = list(refs)
    place_ref, order_ref = refs[:2]
    q_refs = refs[2:6]
    msgs = refs[6 : 6 + len(steps)]
    refs = refs[6 + len(steps) :]
    if not first:
        m_in, l_in, acc_in = refs[:3]
        refs = refs[3:]
    if last:
        outs = refs[:4]
        refs = refs[4:]
    else:
        m_out, l_out, acc_out = refs[:3]
        refs = refs[3:]
    qx, kx, vx, s_a, s_b, m_s, l_s, acc_s, where = refs
    x, yl, z, offset = place_ref[0], place_ref[1], place_ref[2], place_ref[3]
    n_blocks = 4 * len(steps)

    token = lax.broadcasted_iota(jnp.int32, (BLK, D), 0)
    column = lax.broadcasted_iota(jnp.int32, (BLK, D), 1)
    hidden = ((column < BLK) & (column > token)) | (column == BLK)
    q_extra = jnp.where(hidden, NEG, 0.0).astype(jnp.bfloat16)
    own_rows = jnp.where(column == token, 1.0, 0.0).astype(jnp.bfloat16)
    for g in range(4):
        for b in range(2):
            for h in range(HEADS):
                rows = slice(h * BLK, (h + 1) * BLK)
                qx[2 * g + b, rows, :D] = q_refs[g][b * BLK : (b + 1) * BLK, h * D : (h + 1) * D]
                qx[2 * g + b, rows, D:] = q_extra
    kx[...] = jnp.zeros_like(kx)
    vx[...] = jnp.zeros_like(vx)

    ctxs = []
    for step in steps:
        zz = lax.rem(z + step + 8, 8)
        ctxs += [x * 16 + yl * 8 + zz, (3 - x) * 16 + yl * 8 + zz]
    cache_rows = jnp.int32(0)
    slot = lax.broadcasted_iota(jnp.int32, (CACHE, D), 0)
    lane = lax.broadcasted_iota(jnp.int32, (CACHE, D), 1)
    for j, ctx in enumerate(ctxs):
        filled = offset - ctx * CACHE
        src = msgs[j // 2]
        base = (j % 2) * SHARD

        @pl.when(filled > 0)
        def _(src=src, base=base, at=cache_rows, filled=filled):
            to = pl.ds(pl.multiple_of(at, CACHE), CACHE)
            kx[to, :D] = src[base + TOK : base + TOK + CACHE, :]
            kx[to, D:] = jnp.where((slot >= filled) & (lane == BLK), 1.0, 0.0).astype(jnp.bfloat16)
            vx[to, :] = src[base + 2 * TOK + CACHE : base + SHARD, :]

        cache_rows = cache_rows + jnp.where(filled > 0, CACHE, 0)

    ids = [order_ref[2 * ctx + b] for ctx in ctxs for b in range(2)]
    for j, mine in enumerate(ids):
        where[j] = mine
        rank = jnp.int32(0)
        for k, other in enumerate(ids):
            if k != j:
                rank = rank + (other < mine).astype(jnp.int32)
        to = pl.ds(pl.multiple_of(cache_rows + rank * BLK, 32), BLK)
        src = msgs[j // 4]
        base = ((j // 2) % 2) * SHARD + (j % 2) * BLK
        kx[to, :D] = src[base : base + BLK, :]
        vx[to, :] = src[base + TOK + CACHE : base + TOK + CACHE + BLK, :]

    pad_lane = lax.broadcasted_iota(jnp.int32, (TILE, D), 1)
    pad_rows = jnp.where(pad_lane == BLK, 1.0, 0.0).astype(jnp.bfloat16)

    def scores(qb, i):
        keys = kx[pl.ds(pl.multiple_of(i * TILE, TILE), TILE), :]
        return lax.dot_general(keys, qx[qb], NT, preferred_element_type=jnp.float32)

    def absorb(s_ref, i):
        s = s_ref[...]
        m0 = m_s[...]
        m1 = jnp.maximum(m0, jnp.max(s, axis=0, keepdims=True) * SCALE)
        factor = jnp.exp2(m0 - m1)
        p = jnp.exp2(s * SCALE - m1[:1])
        l_s[...] = l_s[...] * factor + jnp.sum(p, axis=0, keepdims=True)
        m_s[...] = m1
        values = vx[pl.ds(pl.multiple_of(i * TILE, TILE), TILE), :]
        acc_s[...] = acc_s[...] * factor[:1] + lax.dot_general(
            values, p.astype(jnp.bfloat16), TN, preferred_element_type=jnp.float32
        )

    def block(qb, carry):
        g, b = qb // 2, qb % 2
        gx, gy = g % 2, g // 2
        q_ctx = (x + gx - 2 * gx * lax.rem(x, 2)) * 16 + (yl + gy - 2 * gy * yl) * 8 + z
        q_id = order_ref[2 * q_ctx + b]
        count = jnp.int32(0)
        own = jnp.int32(0)
        for j in range(n_blocks):
            count = count + (where[j] <= q_id).astype(jnp.int32)
            own = own + (where[j] == q_id).astype(jnp.int32)
        end = cache_rows + count * BLK
        tiles = (end + TILE - 1) // TILE
        if first:
            m_s[...] = jnp.full_like(m_s, NEG)
            l_s[...] = jnp.zeros_like(l_s)
            acc_s[...] = jnp.zeros_like(acc_s)
        else:
            m_s[...] = m_in[qb]
            l_s[...] = l_in[qb]
            acc_s[...] = acc_in[qb]
        tail = pl.ds(pl.multiple_of(end, 32), TILE)
        kx[tail, D:] = pad_rows

        @pl.when(own > 0)
        def _():
            kx[pl.ds(pl.multiple_of(jnp.maximum(end - BLK, 0), 32), BLK), D:] = own_rows

        @pl.when(tiles > 0)
        def _():
            s_a[...] = scores(qb, 0)

            def pair(j, c):
                i = 2 * j
                s_b[...] = scores(qb, i + 1)
                absorb(s_a, i)
                s_a[...] = scores(qb, i + 2)
                absorb(s_b, i + 1)
                return c

            lax.fori_loop(0, (tiles - 1) // 2, pair, 0)

            @pl.when(tiles % 2 == 0)
            def _():
                s_b[...] = scores(qb, tiles - 1)
                absorb(s_a, tiles - 2)
                absorb(s_b, tiles - 1)

            @pl.when(tiles % 2 == 1)
            def _():
                absorb(s_a, tiles - 1)

        kx[tail, D:] = jnp.zeros_like(pad_rows)

        @pl.when(own > 0)
        def _():
            kx[pl.ds(pl.multiple_of(jnp.maximum(end - BLK, 0), 32), BLK), D:] = jnp.zeros_like(own_rows)

        if last:
            total = l_s[...]
            some = total > 0.0
            safe = jnp.where(some, total, 1.0)
            value = (acc_s[...] / safe[:1]).astype(jnp.bfloat16)
            logsum = jnp.where(some, m_s[...] + jnp.log2(safe), NEG)
            high = logsum.astype(jnp.bfloat16)
            rest = logsum - high.astype(jnp.float32)
            mid = rest.astype(jnp.bfloat16)
            low = (rest - mid.astype(jnp.float32)).astype(jnp.bfloat16)
            row = lax.broadcasted_iota(jnp.int32, (16, ROWS), 0)
            h2 = jnp.concatenate([high, high], 0).astype(jnp.float32)
            m2 = jnp.concatenate([mid, mid], 0).astype(jnp.float32)
            l2 = jnp.concatenate([low, low], 0).astype(jnp.float32)
            pieces = jnp.where(row == 0, h2, jnp.where(row == 1, m2, l2)).astype(jnp.bfloat16)
            for gg in range(4):

                @pl.when(g == gg)
                def _(gg=gg):
                    outs[gg][b, :D, :] = value
                    outs[gg][b, D:, :] = pieces
        else:
            m_out[qb] = m_s[...]
            l_out[qb] = l_s[...]
            acc_out[qb] = acc_s[...]
        return carry

    lax.fori_loop(0, 8, block, 0)


def run_chunk(steps, state, last, place, order, queries, messages):
    first = state is None
    keep = 256 * 2 * len(steps) + TILE
    sds = jax.ShapeDtypeStruct
    state_shapes = (
        sds((8, 8, ROWS), jnp.float32),
        sds((8, 8, ROWS), jnp.float32),
        sds((8, D, ROWS), jnp.float32),
    )
    smem = pl.BlockSpec(memory_space=pltpu.SMEM)
    vmem = pl.BlockSpec(memory_space=VMEM)
    operands = [place, order, *queries, *messages] + ([] if first else list(state))
    out_shape = (sds((2, OUT_ROWS, ROWS), jnp.bfloat16),) * 4 if last else state_shapes
    work = 2 * len(steps)
    aliases = {}
    if not first and not last:
        aliases = {len(operands) - 3 + i: i for i in range(3)}
    return pl.pallas_call(
        functools.partial(attend_chunk, tuple(steps), first, last),
        out_shape=out_shape,
        in_specs=[smem, smem] + [vmem] * (len(operands) - 2),
        out_specs=(vmem,) * len(out_shape),
        scratch_shapes=[
            VMEM((8, ROWS, 2 * D), jnp.bfloat16),
            VMEM((keep, 2 * D), jnp.bfloat16),
            VMEM((keep, D), jnp.bfloat16),
            VMEM((TILE, ROWS), jnp.float32),
            VMEM((TILE, ROWS), jnp.float32),
            VMEM((8, ROWS), jnp.float32),
            VMEM((8, ROWS), jnp.float32),
            VMEM((D, ROWS), jnp.float32),
            pltpu.SMEM((2 * work,), jnp.int32),
        ],
        input_output_aliases=aliases,
        compiler_params=pltpu.CompilerParams(vmem_limit_bytes=48 * 2**20),
        cost_estimate=pl.CostEstimate(
            flops=work * 1024 * 1024 * 1024, bytes_accessed=8 * 2**20, transcendentals=work * 10**6
        ),
        name=f"attend_{len(steps)}_{int(first)}{int(last)}",
    )(*operands)


def merge_body(*refs):
    parts, out = refs[:4], refs[4]
    for b in range(2):
        logs = []
        for part in parts:
            row = part[b, D:, :].astype(jnp.float32)
            logs.append(row[0:1] + row[1:2] + row[2:3])
        top = functools.reduce(jnp.maximum, logs)
        weights = [jnp.exp2(v - top) for v in logs]
        share = 1.0 / sum(weights)
        mixed = sum(part[b, :D, :].astype(jnp.float32) * (w * share) for part, w in zip(parts, weights))
        for h in range(HEADS):
            out[b * BLK : (b + 1) * BLK, h * D : (h + 1) * D] = mixed[:, h * BLK : (h + 1) * BLK].T.astype(
                jnp.bfloat16
            )


def merge(parts):
    vmem = pl.BlockSpec(memory_space=VMEM)
    return pl.pallas_call(
        merge_body,
        out_shape=jax.ShapeDtypeStruct((TOK, HEADS * D), jnp.bfloat16),
        in_specs=[vmem] * 4,
        out_specs=vmem,
        name="merge",
    )(*parts)


def on_device(queries, window_keys, window_values, stored_keys, stored_values, block_order, window_offset, out_weight):
    x, yl, z = lax.axis_index("x"), lax.axis_index("yl"), lax.axis_index("z")
    place = jnp.stack([x, yl, z, window_offset[0]]).astype(jnp.int32)
    shard = jnp.concatenate([window_keys, stored_keys, window_values, stored_values], 0)

    def along(array, axis, size, to):
        return lax.ppermute(array, axis, [(i, to(i)) for i in range(size)])

    other = along(shard, "x", 4, lambda i: 3 - i)
    base = jnp.concatenate([shard, other], 0)
    pair = [(a, b) for a in range(4) for b in range(2)]
    both = [(2 * a + b, 2 * (a ^ 1) + (1 - b)) for a, b in pair]
    q_sets = [
        queries,
        along(queries, "x", 4, lambda i: i ^ 1),
        along(queries, "yl", 2, lambda i: 1 - i),
        lax.ppermute(queries, ("x", "yl"), both),
    ]
    up = lambda a: along(a, "z", 8, lambda i: (i + 1) % 8)
    down = lambda a: along(a, "z", 8, lambda i: (i - 1) % 8)
    a1, b1 = up(base), down(base)
    a2, b2 = up(a1), down(b1)
    a3, b3 = up(a2), down(b2)
    far = jnp.concatenate([up(a3[:SHARD]), down(b3[SHARD:])], 0)
    state = run_chunk((0, -1, 1), None, False, place, block_order, q_sets, (base, a1, b1))
    state = run_chunk((-2, 2, -3, 3), state, False, place, block_order, q_sets, (a2, b2, a3, b3))
    parts = run_chunk((4,), state, True, place, block_order, q_sets, (far,))
    parts = [
        parts[0],
        along(parts[1], "x", 4, lambda i: i ^ 1),
        along(parts[2], "yl", 2, lambda i: 1 - i),
        lax.ppermute(parts[3], ("x", "yl"), both),
    ]
    attended = merge(parts)
    partial = jnp.dot(attended, out_weight, preferred_element_type=jnp.float32).reshape(2, 2, TOK // 4, -1)
    core, yh = lax.axis_index("core"), lax.axis_index("yh")
    give = lax.dynamic_index_in_dim(partial, 1 - core, 1, keepdims=False).astype(jnp.bfloat16)
    mine = lax.dynamic_index_in_dim(partial, core, 1, keepdims=False)
    mine = mine + along(give, "core", 2, lambda i: 1 - i).astype(jnp.float32)
    give = lax.dynamic_index_in_dim(mine, 1 - yh, 0, keepdims=False).astype(jnp.bfloat16)
    mine = lax.dynamic_index_in_dim(mine, yh, 0, keepdims=False)
    return (mine + along(give, "yh", 2, lambda i: 1 - i).astype(jnp.float32)).astype(jnp.bfloat16)


def solution(mesh):
    fine = Mesh(mesh.devices.reshape(4, 2, 8, 2, 2), ("x", "yl", "z", "yh", "core"))
    ctx, tp = ("x", "yl", "z"), ("yh", "core")
    return jax.shard_map(
        on_device,
        mesh=fine,
        in_specs=(P(ctx, tp),) * 5 + (P(), P(), P(tp, None)),
        out_specs=P((*ctx, *tp), None),
        check_vma=False,
    )
```

time: 1080 us -> 132 us (0.12)
  waiting for transfers between devices: 660 us -> 35.1 us
  matrix products: 213 us -> 5.32 us
  other arithmetic: 161 us -> 4.18 us
  Pallas kernels: 0 us -> 45 us
  starting transfers between devices: 0.09 us -> 30.6 us
  between operations: 14.5 us -> 0.8 us
  local copies, waits for them, and re-layouts: 21.6 us -> 10.1 us
    all_gather x2 -> x0, waiting for transfers between devices: 563 us -> none  [the longest x1 303 us: on_device(): value_rows = lax.all_gather(stacked_values, 'ctx', axis=0, tiled=True)]
    dot_general x128 -> x0, matrix products: 207 us -> none  [the longest x64 113 us: attend(): jnp.einsum('grn,ngd->grd', weights.astype(jnp.bfloat16), value_heads, pre...]
    psum x1 -> x0, waiting for transfers between devices: 96.8 us -> none  [on_device(): lax.psum(jnp.dot(attended, out_weight, preferred_element_type=jnp.float32...]
    reduce_sum x64 -> x0, other arithmetic: 68.2 us -> none  [the longest x32 39.8 us: attend(): new_sum = run_sum * factor + jnp.sum(weights, axis=-1)]
    pallas_call x0 -> x4, Pallas kernels: none -> 45 us  [the longest x3 42.1 us: run_chunk(): pl.pallas_call(functools.partial(attend_chunk, tuple(steps), first, last)...]
    add x160 -> x1, other arithmetic: 44.5 us -> 1.28 us  [on_device(): mine = mine + along(give, 'core', 2, lambda i: 1 - i).astype(jnp.float32)]
    lt x32 -> x0, other arithmetic: 41.9 us -> none  [visibility(): cache_pos < offset]
    ppermute x0 -> x17, waiting for transfers between devices: none -> 35.1 us  [the longest x15 21.7 us: along(): return lax.ppermute(array, axis, [(i, to(i)) for i in range(size)])]
  transfers between devices with their start and end apart: 3 -> 17, of which waited for: 3 -> 8; matrix products, arithmetic and copies ran while one was open for 0% -> 2% of each run, Pallas kernels for 0% -> 23%
where the time goes in v1:
time: 132 us; the launch traced here: 131 us
  Pallas kernels  45 us (34%)
  waiting for transfers between devices  35.1 us (27%)
  starting transfers between devices  30.6 us (23%)
  local copies, waits for them, and re-layouts  10.1 us (8%)
  matrix products  5.32 us (4%)
  other arithmetic  4.18 us (3%)
    pallas_call x3, Pallas kernels, run_chunk(): pl.pallas_call(functools.partial(attend_chunk, tuple(steps), first, last)...  42.1 us
    ppermute x15, starting transfers between devices, along(): return lax.ppermute(array, axis, [(i, to(i)) for i in range(size)])  26.6 us
    ppermute x15, waiting for transfers between devices, along(): return lax.ppermute(array, axis, [(i, to(i)) for i in range(size)])  21.7 us
    unnamed x20, local copies, waits for them, and re-layouts  9.04 us
    ppermute x1, waiting for transfers between devices, on_device(): lax.ppermute(parts[3], ('x', 'yl'), both)  8.9 us
    dot_general x1, matrix products, on_device(): jnp.dot(attended, out_weight, preferred_element_type=jnp.float32)  5.32 us
    ppermute x1, waiting for transfers between devices, on_device(): lax.ppermute(queries, ('x', 'yl'), both)  4.51 us
    pallas_call x1, Pallas kernels, merge(): pl.pallas_call(merge_body, out_shape=jax.ShapeDtypeStruct((TOK, HEADS * D...  2.92 us
  transfers between devices with their start and end apart: 17, of which 8 were waited for; matrix products, arithmetic and copies ran while one was open for 2% of the time, Pallas kernels for 23%

profile of v1, /device:TPU:1, one launch (start us, length us, event | category | flops | bytes accessed | tf_op | source)
XLA Modules:
  0.0 131.1 jit_solution(14593770899764321948)
XLA Ops:
  0.0 0.9 pad_maximum_fusion.1
  0.9 3.4 %collective-permute-start.3 = (bf16[512,128]{1,0:T(8,128)(2,1)S(1)}, bf16[512,128]{1,0:T(8,128)(2,1)S(1)}, u32[]{:S(2)}, u32[]{:S(2)}) collective-permute-start(bf16[512,128]{1,0:T(8,128)(2,1)S(1)} %pad_maximum_fusion.1), channel_id=1, source_target_pairs={{0,192},{64,128},{128,64},{192,0},{1,193},{65,129},{129,65},{193,1... | collective-permute-start | bytes 393224 | tf_op jit(solution)/shard_map/ppermute | solution.py:276
  4.3 0.8 constant_dynamic-update-slice_fusion.4
  5.1 0.7 constant_dynamic-update-slice_fusion.3
  5.8 0.8 constant_dynamic-update-slice_fusion.2
  6.6 0.7 constant_dynamic-update-slice_fusion.1
  7.3 0.0 collective-permute-done.3
  7.3 5.7 %collective-permute-start.8 = (bf16[1024,128]{1,0:T(8,128)(2,1)S(1)}, bf16[1024,128]{1,0:T(8,128)(2,1)S(1)}, u32[]{:S(2)}, u32[]{:S(2)}) collective-permute-start(bf16[1024,128]{1,0:T(8,128)(2,1)S(1)} %constant_dynamic-update-slice_fusion.refs_6_), channel_id=1, source_target_pairs={{0,28},{4,0},{8,4},{12,8},{16,12},{20,16},{24,20},{28,24},{1,29},{... | collective-permute-start | bytes 786440 | tf_op jit(solution)/shard_map/ppermute | solution.py:276
  13.0 0.0 collective-permute-start.4
  13.0 0.0 collective-permute-start
  13.0 1.3 collective-permute-start.1
  14.3 1.3 %collective-permute-start.2 = (bf16[192,1024]{1,0:T(8,128)(2,1)}, bf16[192,1024]{1,0:T(8,128)(2,1)S(1)}, u32[]{:S(2)}, u32[]{:S(2)}) collective-permute-start(bf16[192,1024]{1,0:T(8,128)(2,1)} %refs_2_.5), channel_id=1, source_target_pairs={{0,96},{32,64},{64,32},{96,0},{128,224},{160,192},{192,160},{224,1... | collective-permute-start | bytes 1179656 | tf_op jit(solution)/shard_map/ppermute | solution.py:286
  15.7 1.4 %collective-permute-done.8.refs_8_ = bf16[1024,128]{1,0:T(8,128)(2,1)S(1)} collective-permute-done((bf16[1024,128]{1,0:T(8,128)(2,1)S(1)}, bf16[1024,128]{1,0:T(8,128)(2,1)S(1)}, u32[]{:S(2)}, u32[]{:S(2)}) %collective-permute-start.8) | collective-permute-done | bytes 262176 | tf_op jit(solution)/shard_map/ppermute | solution.py:276
  17.1 3.4 %collective-permute-start.9 = (bf16[1024,128]{1,0:T(8,128)(2,1)S(1)}, bf16[1024,128]{1,0:T(8,128)(2,1)S(1)}, u32[]{:S(2)}, u32[]{:S(2)}) collective-permute-start(bf16[1024,128]{1,0:T(8,128)(2,1)S(1)} %collective-permute-done.8.refs_8_), channel_id=1, source_target_pairs={{0,28},{4,0},{8,4},{12,8},{16,12},{20,16},{24,20},{28,24},{1,29},{... | collective-permute-start | bytes 786440 | tf_op jit(solution)/shard_map/ppermute | solution.py:276
  20.5 0.0 collective-permute-done.4.refs_7_
  20.5 0.0 collective-permute-start.5
  21.2 0.1 pad_add_fusion.refs_0_
  21.2 2.6 %collective-permute-done.9.refs_7_ = bf16[1024,128]{1,0:T(8,128)(2,1)S(1)} collective-permute-done((bf16[1024,128]{1,0:T(8,128)(2,1)S(1)}, bf16[1024,128]{1,0:T(8,128)(2,1)S(1)}, u32[]{:S(2)}, u32[]{:S(2)}) %collective-permute-start.9) | collective-permute-done | bytes 262176 | tf_op jit(solution)/shard_map/ppermute | solution.py:276
  23.8 3.1 %collective-permute-start.10 = (bf16[1024,128]{1,0:T(8,128)(2,1)S(1)}, bf16[1024,128]{1,0:T(8,128)(2,1)S(1)}, u32[]{:S(2)}, u32[]{:S(2)}) collective-permute-start(bf16[1024,128]{1,0:T(8,128)(2,1)S(1)} %collective-permute-done.9.refs_7_), channel_id=1, source_target_pairs={{0,28},{4,0},{8,4},{12,8},{16,12},{20,16},{24,20},{28,24},{1,29},{... | collective-permute-start | bytes 786440 | tf_op jit(solution)/shard_map/ppermute | solution.py:276
  26.9 0.0 collective-permute-done.5.refs_6_
  26.9 0.0 collective-permute-start.6
  26.9 0.0 collective-permute-done.refs_3_
  26.9 0.0 collective-permute-done.1.refs_4_
  27.0 4.5 %collective-permute-done.2.refs_5_ = bf16[192,1024]{1,0:T(8,128)(2,1)S(1)} collective-permute-done((bf16[192,1024]{1,0:T(8,128)(2,1)}, bf16[192,1024]{1,0:T(8,128)(2,1)S(1)}, u32[]{:S(2)}, u32[]{:S(2)}) %collective-permute-start.2) | collective-permute-done | bytes 393248 | tf_op jit(solution)/shard_map/ppermute | solution.py:286
  31.5 0.0 copy-start.1
  31.5 1.0 copy-done.1
  32.5 0.0 copy-start.2
  32.5 0.7 copy-done.2
  33.1 14.5 %attend_3_10.1 = (f32[8,8,768]{2,1,0:T(8,128)S(1)}, f32[8,8,768]{2,1,0:T(8,128)S(1)}, f32[8,128,768]{2,1,0:T(8,128)S(1)}) custom-call(s32[4]{0:T(128)S(1)} %pad_add_fusion.refs_0_, s32[128]{0:T(128)S(1)} %copy-done.2, bf16[192,1024]{1,0:T(8,128)(2,1)S(1)} %copy-done.1, bf16[192,1024]{1,0:T(8,128)(2,1)S(1)} %collective-permute-done.refs_3_, ...), custom_call_target="tpu_custom_call" | custom-call | flops 6442450944 | bytes 8388608 | tf_op jit(solution)/shard_map/attend_3_10/pallas_call | solution.py:217
  47.7 0.0 collective-permute-done.10.refs_9_
  47.7 2.2 %collective-permute-start.11 = (bf16[512,128]{1,0:T(8,128)(2,1)S(1)}, bf16[512,128]{1,0:T(8,128)(2,1)S(1)}, u32[]{:S(2)}, u32[]{:S(2)}) collective-permute-start(bf16[512,128]{1,0:T(8,128)(2,1)S(1)} %slice.9), channel_id=1, source_target_pairs={{0,28},{4,0},{8,4},{12,8},{16,12},{20,16},{24,20},{28,24},{1,29},{... | collective-permute-start | bytes 393224 | tf_op jit(solution)/shard_map/ppermute | solution.py:276
  49.9 0.0 collective-permute-done.6.refs_8_
  49.9 0.3 collective-permute-start.7
  50.2 16.2 %attend_4_00.1 = (f32[8,8,768]{2,1,0:T(8,128)S(1)}, f32[8,8,768]{2,1,0:T(8,128)S(1)}, f32[8,128,768]{2,1,0:T(8,128)S(1)}) custom-call(s32[4]{0:T(128)S(1)} %pad_add_fusion.refs_0_, s32[128]{0:T(128)S(1)} %copy-done.2, bf16[192,1024]{1,0:T(8,128)(2,1)S(1)} %copy-done.1, ...), custom_call_target="tpu_custom_call", output_to_operand_aliasing={{0}: (10, {}), {1}: (11, {}), {2}: (12, {})} | custom-call | flops 8589934592 | bytes 8388608 | tf_op jit(solution)/shard_map/attend_4_00/pallas_call | solution.py:217
  66.4 0.0 copy-start.3
  66.4 1.6 %copy-done.3 = f32[8,128,768]{2,1,0:T(8,128)} copy-done((f32[8,128,768]{2,1,0:T(8,128)}, f32[8,128,768]{2,1,0:T(8,128)S(1)}, u32[]{:S(2)}) %copy-start.3) | copy-done | bytes 3145752
  68.0 0.0 collective-permute-done.11
  68.0 0.0 collective-permute-done.7
  68.1 11.4 %attend_1_01.1 = (bf16[2,144,768]{2,1,0:T(8,128)(2,1)S(1)}, bf16[2,144,768]{2,1,0:T(8,128)(2,1)S(1)}, bf16[2,144,768]{2,1,0:T(8,128)(2,1)S(1)}, bf16[2,144,768]{2,1,0:T(8,128)(2,1)S(1)}) custom-call(s32[4]{0:T(128)S(1)} %pad_add_fusion.refs_0_, s32[128]{0:T(128)S(1)} %copy-done.2, bf16[192,1024]{1,0:T(8,128)(2,1)S(1)} %copy-done.1, ...), custom_call_target="tpu_custom_call" | custom-call | flops 2147483648 | bytes 8388608 | tf_op jit(solution)/shard_map/attend_1_01/pallas_call | solution.py:217
  79.4 0.0 copy-start
  79.4 0.8 copy-done
  80.2 0.0 collective-permute-start.12
  80.2 0.0 collective-permute-start.13
  80.2 2.6 %collective-permute-start.14 = (bf16[2,144,768]{2,1,0:T(8,128)(2,1)S(1)}, bf16[2,144,768]{2,1,0:T(8,128)(2,1)S(1)}, u32[]{:S(2)}, u32[]{:S(2)}) collective-permute-start(bf16[2,144,768]{2,1,0:T(8,128)(2,1)S(1)} %get-tuple-element.24), channel_id=1, source_target_pairs={{0,96},{32,64},{64,32},{96,0},{128,224},{160,192},{192,160},{224,1... | collective-permute-start | bytes 1327112 | tf_op jit(solution)/shard_map/ppermute | solution.py:301
  82.8 5.7 %collective-permute-done.12.refs_1_ = bf16[2,144,768]{2,1,0:T(8,128)(2,1)S(1)} collective-permute-done((bf16[2,144,768]{2,1,0:T(8,128)(2,1)S(1)}, bf16[2,144,768]{2,1,0:T(8,128)(2,1)S(1)}, u32[]{:S(2)}, u32[]{:S(2)}) %collective-permute-start.12) | collective-permute-done | bytes 442400 | tf_op jit(solution)/shard_map/ppermute | solution.py:276
  88.5 0.0 copy-start.5
  88.6 0.3 collective-permute-done.13.refs_2_
  88.9 0.0 copy-start.6
  88.9 8.9 %collective-permute-done.14.refs_3_ = bf16[2,144,768]{2,1,0:T(8,128)(2,1)S(1)} collective-permute-done((bf16[2,144,768]{2,1,0:T(8,128)(2,1)S(1)}, bf16[2,144,768]{2,1,0:T(8,128)(2,1)S(1)}, u32[]{:S(2)}, u32[]{:S(2)}) %collective-permute-start.14) | collective-permute-done | bytes 442400 | tf_op jit(solution)/shard_map/ppermute | solution.py:301
  97.8 0.0 copy-start.7
  97.8 0.0 copy-done.5
  97.8 0.0 copy-done.6
  97.8 0.8 copy-done.7
  98.5 2.9 %merge.1 = bf16[192,1024]{1,0:T(8,128)(2,1)} custom-call(bf16[2,144,768]{2,1,0:T(8,128)(2,1)} %copy-done, bf16[2,144,768]{2,1,0:T(8,128)(2,1)} %copy-done.5, bf16[2,144,768]{2,1,0:T(8,128)(2,1)} %copy-done.6, bf16[2,144,768]{2,1,0:T(8,128)(2,1)} %copy-done.7), custom_call_target="tpu_custom_call" | custom-call | tf_op jit(solution)/shard_map/merge/pallas_call | solution.py:261
  101.4 5.3 %fusion.3 = f32[192,4096]{1,0:T(8,128)S(1)} fusion(bf16[192,1024]{1,0:T(8,128)(2,1)} %merge.1, bf16[1024,4096]{1,0:T(8,128)(2,1)} %param.15), kind=kOutput, calls=%fused_computation.15 | convolution fusion | flops 1610612736 | bytes 11927552 | tf_op jit(solution)/shard_map/dot_general | solution.py:304
  106.8 1.0 fusion
  107.8 4.7 %collective-permute-start.15 = (bf16[2,48,4096]{2,1,0:T(8,128)(2,1)}, bf16[2,48,4096]{2,1,0:T(8,128)(2,1)}, u32[]{:S(2)}, u32[]{:S(2)}) collective-permute-start(bf16[2,48,4096]{2,1,0:T(8,128)(2,1)} %fusion), channel_id=1, source_target_pairs={{0,1},{1,0},{2,3},{3,2},{4,5},{5,4},{6,7},{7,6},{8,9},{9,8},{10,11... | collective-permute-start | bytes 2359304 | tf_op jit(solution)/shard_map/ppermute | solution.py:276
  112.5 2.3 %collective-permute-done.15 = bf16[2,48,4096]{2,1,0:T(8,128)(2,1)} collective-permute-done((bf16[2,48,4096]{2,1,0:T(8,128)(2,1)}, bf16[2,48,4096]{2,1,0:T(8,128)(2,1)}, u32[]{:S(2)}, u32[]{:S(2)}) %collective-permute-start.15) | collective-permute-done | bytes 786464 | tf_op jit(solution)/shard_map/ppermute | solution.py:276
  114.7 1.3 bitcast_add_fusion
  116.0 0.0 copy-start.4
  116.0 1.2 copy-done.4
  117.2 2.5 %collective-permute-start.16 = (bf16[48,4096]{1,0:T(8,128)(2,1)S(1)}, bf16[48,4096]{1,0:T(8,128)(2,1)S(1)}, u32[]{:S(2)}, u32[]{:S(2)}) collective-permute-start(bf16[48,4096]{1,0:T(8,128)(2,1)S(1)} %fusion.2), channel_id=1, source_target_pairs={{0,2},{2,0},{1,3},{3,1},{4,6},{6,4},{5,7},{7,5},{8,10},{10,8},{9,1... | collective-permute-start | bytes 1179656 | tf_op jit(solution)/shard_map/ppermute | solution.py:276
  119.7 9.4 %collective-permute-done.16 = bf16[48,4096]{1,0:T(8,128)(2,1)S(1)} collective-permute-done((bf16[48,4096]{1,0:T(8,128)(2,1)S(1)}, bf16[48,4096]{1,0:T(8,128)(2,1)S(1)}, u32[]{:S(2)}, u32[]{:S(2)}) %collective-permute-start.16) | collective-permute-done | bytes 393248 | tf_op jit(solution)/shard_map/ppermute | solution.py:276
  129.2 1.9 %fusion.1 = bf16[48,4096]{1,0:T(8,128)(2,1)} fusion(bf16[48,4096]{1,0:T(8,128)(2,1)S(1)} %collective-permute-done.16, f32[2,48,4096]{2,1,0:T(8,128)} %copy-done.4, s32[]{:T(128)S(6)} %select_n.16), kind=kLoop, calls=%fused_computation.4 | loop fusion | flops 589824 | bytes 1572868 | tf_op jit(solution)/shard_map/convert_element_type | solution.py:311
  (5 shorter events, 0.1 us)
Async XLA Ops:
  0.9 6.5 %collective-permute-start.3 = (bf16[512,128]{1,0:T(8,128)(2,1)S(1)}, bf16[512,128]{1,0:T(8,128)(2,1)S(1)}, u32[]{:S(2)}, u32[]{:S(2)}) collective-permute-start(bf16[512,128]{1,0:T(8,128)(2,1)S(1)} %pad_maximum_fusion.1), channel_id=1, source_target_pairs={{0,192},{64,128},{128,64},{192,0},{1,193},{65,129},{129,65},{193,1... | collective-permute-start | bytes 393224 | tf_op jit(solution)/shard_map/ppermute | solution.py:276
  7.3 9.7 %collective-permute-start.8 = (bf16[1024,128]{1,0:T(8,128)(2,1)S(1)}, bf16[1024,128]{1,0:T(8,128)(2,1)S(1)}, u32[]{:S(2)}, u32[]{:S(2)}) collective-permute-start(bf16[1024,128]{1,0:T(8,128)(2,1)S(1)} %constant_dynamic-update-slice_fusion.refs_6_), channel_id=1, source_target_pairs={{0,28},{4,0},{8,4},{12,8},{16,12},{20,16},{24,20},{28,24},{1,29},{... | collective-permute-start | bytes 786440 | tf_op jit(solution)/shard_map/ppermute | solution.py:276
  13.0 7.5 %collective-permute-start.4 = (bf16[1024,128]{1,0:T(8,128)(2,1)S(1)}, bf16[1024,128]{1,0:T(8,128)(2,1)S(1)}, u32[]{:S(2)}, u32[]{:S(2)}) collective-permute-start(bf16[1024,128]{1,0:T(8,128)(2,1)S(1)} %constant_dynamic-update-slice_fusion.refs_6_), channel_id=1, source_target_pairs={{0,4},{4,8},{8,12},{12,16},{16,20},{20,24},{24,28},{28,0},{1,5},{5... | collective-permute-start | bytes 786440 | tf_op jit(solution)/shard_map/ppermute | solution.py:276
  13.0 13.9 %collective-permute-start = (bf16[192,1024]{1,0:T(8,128)(2,1)}, bf16[192,1024]{1,0:T(8,128)(2,1)S(1)}, u32[]{:S(2)}, u32[]{:S(2)}) collective-permute-start(bf16[192,1024]{1,0:T(8,128)(2,1)} %refs_2_.5), channel_id=1, source_target_pairs={{0,64},{64,0},{128,192},{192,128},{1,65},{65,1},{129,193},{193,129... | collective-permute-start | bytes 1179656 | tf_op jit(solution)/shard_map/ppermute | solution.py:276
  13.0 13.9 %collective-permute-start.1 = (bf16[192,1024]{1,0:T(8,128)(2,1)}, bf16[192,1024]{1,0:T(8,128)(2,1)S(1)}, u32[]{:S(2)}, u32[]{:S(2)}) collective-permute-start(bf16[192,1024]{1,0:T(8,128)(2,1)} %refs_2_.5), channel_id=1, source_target_pairs={{0,32},{32,0},{1,33},{33,1},{2,34},{34,2},{3,35},{35,3},{4,36},{36... | collective-permute-start | bytes 1179656 | tf_op jit(solution)/shard_map/ppermute | solution.py:276
  14.3 17.1 %collective-permute-start.2 = (bf16[192,1024]{1,0:T(8,128)(2,1)}, bf16[192,1024]{1,0:T(8,128)(2,1)S(1)}, u32[]{:S(2)}, u32[]{:S(2)}) collective-permute-start(bf16[192,1024]{1,0:T(8,128)(2,1)} %refs_2_.5), channel_id=1, source_target_pairs={{0,96},{32,64},{64,32},{96,0},{128,224},{160,192},{192,160},{224,1... | collective-permute-start | bytes 1179656 | tf_op jit(solution)/shard_map/ppermute | solution.py:286
  17.1 6.7 %collective-permute-start.9 = (bf16[1024,128]{1,0:T(8,128)(2,1)S(1)}, bf16[1024,128]{1,0:T(8,128)(2,1)S(1)}, u32[]{:S(2)}, u32[]{:S(2)}) collective-permute-start(bf16[1024,128]{1,0:T(8,128)(2,1)S(1)} %collective-permute-done.8.refs_8_), channel_id=1, source_target_pairs={{0,28},{4,0},{8,4},{12,8},{16,12},{20,16},{24,20},{28,24},{1,29},{... | collective-permute-start | bytes 786440 | tf_op jit(solution)/shard_map/ppermute | solution.py:276
  20.5 6.4 %collective-permute-start.5 = (bf16[1024,128]{1,0:T(8,128)(2,1)S(1)}, bf16[1024,128]{1,0:T(8,128)(2,1)S(1)}, u32[]{:S(2)}, u32[]{:S(2)}) collective-permute-start(bf16[1024,128]{1,0:T(8,128)(2,1)S(1)} %collective-permute-done.4.refs_7_), channel_id=1, source_target_pairs={{0,4},{4,8},{8,12},{12,16},{16,20},{20,24},{24,28},{28,0},{1,5},{5... | collective-permute-start | bytes 786440 | tf_op jit(solution)/shard_map/ppermute | solution.py:276
  23.8 23.9 %collective-permute-start.10 = (bf16[1024,128]{1,0:T(8,128)(2,1)S(1)}, bf16[1024,128]{1,0:T(8,128)(2,1)S(1)}, u32[]{:S(2)}, u32[]{:S(2)}) collective-permute-start(bf16[1024,128]{1,0:T(8,128)(2,1)S(1)} %collective-permute-done.9.refs_7_), channel_id=1, source_target_pairs={{0,28},{4,0},{8,4},{12,8},{16,12},{20,16},{24,20},{28,24},{1,29},{... | collective-permute-start | bytes 786440 | tf_op jit(solution)/shard_map/ppermute | solution.py:276
  26.9 23.0 %collective-permute-start.6 = (bf16[1024,128]{1,0:T(8,128)(2,1)S(1)}, bf16[1024,128]{1,0:T(8,128)(2,1)S(1)}, u32[]{:S(2)}, u32[]{:S(2)}) collective-permute-start(bf16[1024,128]{1,0:T(8,128)(2,1)S(1)} %collective-permute-done.5.refs_6_), channel_id=1, source_target_pairs={{0,4},{4,8},{8,12},{12,16},{16,20},{20,24},{24,28},{28,0},{1,5},{5... | collective-permute-start | bytes 786440 | tf_op jit(solution)/shard_map/ppermute | solution.py:276
  31.5 1.0 copy-start.1
  32.5 0.7 copy-start.2
  47.7 20.3 %collective-permute-start.11 = (bf16[512,128]{1,0:T(8,128)(2,1)S(1)}, bf16[512,128]{1,0:T(8,128)(2,1)S(1)}, u32[]{:S(2)}, u32[]{:S(2)}) collective-permute-start(bf16[512,128]{1,0:T(8,128)(2,1)S(1)} %slice.9), channel_id=1, source_target_pairs={{0,28},{4,0},{8,4},{12,8},{16,12},{20,16},{24,20},{28,24},{1,29},{... | collective-permute-start | bytes 393224 | tf_op jit(solution)/shard_map/ppermute | solution.py:276
  49.9 18.1 %collective-permute-start.7 = (bf16[512,128]{1,0:T(8,128)(2,1)S(1)}, bf16[512,128]{1,0:T(8,128)(2,1)S(1)}, u32[]{:S(2)}, u32[]{:S(2)}) collective-permute-start(bf16[512,128]{1,0:T(8,128)(2,1)S(1)} %slice.8), channel_id=1, source_target_pairs={{0,4},{4,8},{8,12},{12,16},{16,20},{20,24},{24,28},{28,0},{1,5},{5... | collective-permute-start | bytes 393224 | tf_op jit(solution)/shard_map/ppermute | solution.py:276
  66.4 1.6 %copy-start.3 = (f32[8,128,768]{2,1,0:T(8,128)}, f32[8,128,768]{2,1,0:T(8,128)S(1)}, u32[]{:S(2)}) copy-start(f32[8,128,768]{2,1,0:T(8,128)S(1)} %get-tuple-element.20.refs_9_) | copy-start | bytes 9437188
  79.4 0.8 copy-start
  80.2 8.3 %collective-permute-start.12 = (bf16[2,144,768]{2,1,0:T(8,128)(2,1)S(1)}, bf16[2,144,768]{2,1,0:T(8,128)(2,1)S(1)}, u32[]{:S(2)}, u32[]{:S(2)}) collective-permute-start(bf16[2,144,768]{2,1,0:T(8,128)(2,1)S(1)} %get-tuple-element.22), channel_id=1, source_target_pairs={{0,64},{64,0},{128,192},{192,128},{1,65},{65,1},{129,193},{193,129... | collective-permute-start | bytes 1327112 | tf_op jit(solution)/shard_map/ppermute | solution.py:276
  80.2 8.7 %collective-permute-start.13 = (bf16[2,144,768]{2,1,0:T(8,128)(2,1)S(1)}, bf16[2,144,768]{2,1,0:T(8,128)(2,1)S(1)}, u32[]{:S(2)}, u32[]{:S(2)}) collective-permute-start(bf16[2,144,768]{2,1,0:T(8,128)(2,1)S(1)} %get-tuple-element.23), channel_id=1, source_target_pairs={{0,32},{32,0},{1,33},{33,1},{2,34},{34,2},{3,35},{35,3},{4,36},{36... | collective-permute-start | bytes 1327112 | tf_op jit(solution)/shard_map/ppermute | solution.py:276
  80.2 17.5 %collective-permute-start.14 = (bf16[2,144,768]{2,1,0:T(8,128)(2,1)S(1)}, bf16[2,144,768]{2,1,0:T(8,128)(2,1)S(1)}, u32[]{:S(2)}, u32[]{:S(2)}) collective-permute-start(bf16[2,144,768]{2,1,0:T(8,128)(2,1)S(1)} %get-tuple-element.24), channel_id=1, source_target_pairs={{0,96},{32,64},{64,32},{96,0},{128,224},{160,192},{192,160},{224,1... | collective-permute-start | bytes 1327112 | tf_op jit(solution)/shard_map/ppermute | solution.py:301
  88.5 9.2 %copy-start.5 = (bf16[2,144,768]{2,1,0:T(8,128)(2,1)}, bf16[2,144,768]{2,1,0:T(8,128)(2,1)S(1)}, u32[]{:S(2)}) copy-start(bf16[2,144,768]{2,1,0:T(8,128)(2,1)S(1)} %collective-permute-done.12.refs_1_) | copy-start | bytes 1327108
  88.9 8.9 %copy-start.6 = (bf16[2,144,768]{2,1,0:T(8,128)(2,1)}, bf16[2,144,768]{2,1,0:T(8,128)(2,1)S(1)}, u32[]{:S(2)}) copy-start(bf16[2,144,768]{2,1,0:T(8,128)(2,1)S(1)} %collective-permute-done.13.refs_2_) | copy-start | bytes 1327108
  97.8 0.8 copy-start.7
  107.8 7.0 %collective-permute-start.15 = (bf16[2,48,4096]{2,1,0:T(8,128)(2,1)}, bf16[2,48,4096]{2,1,0:T(8,128)(2,1)}, u32[]{:S(2)}, u32[]{:S(2)}) collective-permute-start(bf16[2,48,4096]{2,1,0:T(8,128)(2,1)} %fusion), channel_id=1, source_target_pairs={{0,1},{1,0},{2,3},{3,2},{4,5},{5,4},{6,7},{7,6},{8,9},{9,8},{10,11... | collective-permute-start | bytes 2359304 | tf_op jit(solution)/shard_map/ppermute | solution.py:276
  116.0 1.2 copy-start.4
  117.2 11.9 %collective-permute-start.16 = (bf16[48,4096]{1,0:T(8,128)(2,1)S(1)}, bf16[48,4096]{1,0:T(8,128)(2,1)S(1)}, u32[]{:S(2)}, u32[]{:S(2)}) collective-permute-start(bf16[48,4096]{1,0:T(8,128)(2,1)S(1)} %fusion.2), channel_id=1, source_target_pairs={{0,2},{2,0},{1,3},{3,1},{4,6},{6,4},{5,7},{7,5},{8,10},{10,8},{9,1... | collective-permute-start | bytes 1179656 | tf_op jit(solution)/shard_map/ppermute | solution.py:276
